TPU v7x, 512 devices: a whole 4x4x16 slice. The times are simulated.
512 devices in a mesh: row: 64 (over x, z), col: 8 (over y, core).
Axes of the slice: x: 4, y: 4, z: 16, core: 2. Of those that a mesh axis runs over, the one named last changes fastest.
Arguments:
- kelvin_start: float32 [512, 512, 128], P('row', 'col'), may hold values from 1 to 2.5
- mass_ratio: float32 [512, 512, 128], P('row', 'col'), may hold values from 0.6 to 1
- material_region_labels: int32 [512, 512], P('row', 'col'), may hold values from 0 to 7
- pristine_conductivity: float32 [8], replicated, may hold values from 0.5 to 2
- burnt_conductivity: float32 [8], replicated, may hold values from 0.5 to 2
- burnt_mass_ratio: float32 [8], replicated, may hold values from 0.25 to 0.5
- arrhenius_prefactor: float32 [8], replicated, may hold values from 1 to 30
- onset_kelvin: float32 [8], replicated, may hold values from 2 to 6
- exchange_film_strength: float32 [64, 8, 64, 128], P('row', 'col'), may hold values from 0.25 to 4
- stagnation_kelvin: float32 [64, 8, 64, 128], P('row', 'col'), may hold values from 2 to 6
- receiving_element: int32 [64, 8, 64, 128], P('row', 'col'), may hold values from 0 to 511
- occupied_slot_totals: int32 [64, 8, 64], P('row', 'col'), may hold values from 16 to 128, as said below
Outputs:
- kelvin_after: float32 [512, 512, 128], P('row', 'col')
- mass_ratio_after: float32 [512, 512, 128], P('row', 'col')
Inputs may be any that keep to these rules, and one draw needn't show every extreme that they name: `occupied_slot_totals`: live slots come first in each block; in every col one destination tile receives 128 live faces from every source; slots at or past the count hold arbitrary values. `receiving_element`: cell i * 64 + j is row i and column j of the destination tile.
All inputs are finite; a program needn't handle non-finite values.
Results may differ from a plain program's by a relative error of at most 0.0003.
Values sent between devices are 32-bit elements; how exact they have to be, the bound alone decides.
A program may use at most 64 MiB of HBM per device.

v0:
```python
import jax
import jax.numpy as jnp
from jax import lax
from jax.sharding import PartitionSpec as P

R_X = 32
R_Y = 64
R_Z = 1024
EXTERIOR_SHARE = 16


HEAT_OF_PYROLYSIS = 0.3


def take_part(values, first_index, end_index, stride, solve_dim):
    return lax.slice_in_dim(values, first_index, end_index, stride, solve_dim)


def extend_end(values, filler, solve_dim):
    new_shape = list(values.shape)
    new_shape[solve_dim] = 1
    return jnp.concatenate([values, jnp.full(new_shape, filler, values.dtype)], solve_dim)


def merge_halves(even_value, odd_value, odd_count, solve_dim):
    even_head = take_part(even_value, 0, odd_count, 1, solve_dim)
    paired = jnp.stack([even_head, odd_value], solve_dim + 1)
    new_shape = list(even_head.shape)
    new_shape[solve_dim] = 2 * odd_count
    merged = paired.reshape(new_shape)
    return merged


def cyclic_solve(sub_diag, main_diag, super_diag, rights, solve_dim):
    length = main_diag.shape[solve_dim]
    if length == 1:
        return [vector / main_diag for vector in rights]
    odd_count = length // 2
    even_count = length - odd_count
    even_parts = [
        take_part(operand, 0, length, 2, solve_dim) for operand in (sub_diag, main_diag, super_diag)
    ]
    odd_parts = [
        take_part(operand, 1, length, 2, solve_dim) for operand in (sub_diag, main_diag, super_diag)
    ]
    even_rights = [take_part(vector, 0, length, 2, solve_dim) for vector in rights]
    odd_rights = [take_part(vector, 1, length, 2, solve_dim) for vector in rights]
    left_sub, left_main, left_super = [
        take_part(operand, 0, odd_count, 1, solve_dim) for operand in even_parts
    ]
    left_rights = [take_part(vector, 0, odd_count, 1, solve_dim) for vector in even_rights]
    right_sub = take_part(extend_end(even_parts[0], 0.0, solve_dim), 1, odd_count + 1, 1, solve_dim)
    right_main = take_part(
        extend_end(even_parts[1], 1.0, solve_dim), 1, odd_count + 1, 1, solve_dim
    )
    right_super = take_part(
        extend_end(even_parts[2], 0.0, solve_dim), 1, odd_count + 1, 1, solve_dim
    )
    right_rights = [
        take_part(extend_end(vector, 0.0, solve_dim), 1, odd_count + 1, 1, solve_dim)
        for vector in even_rights
    ]
    left_factor = -odd_parts[0] / left_main
    right_factor = -odd_parts[2] / right_main
    reduced_sub = left_factor * left_sub
    reduced_main = odd_parts[1] + left_factor * left_super + right_factor * right_sub
    reduced_super = right_factor * right_super
    reduced_rights = [
        odd_part + left_factor * left_part + right_factor * right_part
        for odd_part, left_part, right_part in zip(odd_rights, left_rights, right_rights)
    ]
    odd_solutions = cyclic_solve(
        reduced_sub, reduced_main, reduced_super, reduced_rights, solve_dim
    )
    results = []
    for even_part, odd_part in zip(even_rights, odd_solutions):
        edge_shape = list(odd_part.shape)
        edge_shape[solve_dim] = 1
        zero_plane = jnp.zeros(edge_shape, odd_part.dtype)
        padded = jnp.concatenate([zero_plane, odd_part, zero_plane], solve_dim)
        before = take_part(padded, 0, even_count, 1, solve_dim)
        after_vals = take_part(padded, 1, even_count + 1, 1, solve_dim)
        even_value = (even_part - even_parts[0] * before - even_parts[2] * after_vals) / even_parts[
            1
        ]
        results.append(merge_halves(even_value, odd_part, odd_count, solve_dim))
    return results


def sweep_coefficients(capacity, diffuse_thermal_energy, diffusion, solve_dim):
    length = diffuse_thermal_energy.shape[solve_dim]
    face_cond = 0.5 * (
        take_part(diffuse_thermal_energy, 0, length - 1, 1, solve_dim)
        + take_part(diffuse_thermal_energy, 1, length, 1, solve_dim)
    )
    edge_shape = list(diffuse_thermal_energy.shape)
    edge_shape[solve_dim] = 1
    zero_edge = jnp.zeros(edge_shape, diffuse_thermal_energy.dtype)
    sub_diag = -diffusion * jnp.concatenate([zero_edge, face_cond], solve_dim)
    super_diag = -diffusion * jnp.concatenate([face_cond, zero_edge], solve_dim)
    main_diag = capacity - sub_diag - super_diag
    return (sub_diag, main_diag, super_diag)


def solve_lines(pieces, diffusion, solve_dim):
    sub_diag, main_diag, super_diag = sweep_coefficients(pieces[1], pieces[2], diffusion, solve_dim)
    return cyclic_solve(sub_diag, main_diag, super_diag, [pieces[0]], solve_dim)[0]


def column_values(material_region_labels, property_arrays):
    matches = (
        material_region_labels[..., None]
        == jnp.arange(property_arrays[0].shape[0], dtype=jnp.int32)
    ).astype(jnp.float32)
    return [jnp.sum(matches * lookup, axis=-1)[..., None] for lookup in property_arrays]


def decompose_through_layers(
    kelvin_start,
    mass_ratio,
    material_region_labels,
    property_arrays,
    exterior_multiplier,
    exterior_flux_amount,
):
    virgin, charred, residue, rate_col, energy = column_values(
        material_region_labels, property_arrays
    )
    old_conduct = charred + (virgin - charred) * (mass_ratio - residue) / (1.0 - residue)
    thickness_dimension = kelvin_start.ndim - 1
    sub_diag, main_diag, super_diag = sweep_coefficients(
        mass_ratio, old_conduct, float(R_Z), thickness_dimension
    )
    main_diag = main_diag.at[..., 0].add(float(EXTERIOR_SHARE) * exterior_multiplier)
    forcing_vector = (
        (mass_ratio * kelvin_start).at[..., 0].add(float(EXTERIOR_SHARE) * exterior_flux_amount)
    )
    depth_temp = cyclic_solve(
        sub_diag, main_diag, super_diag, [forcing_vector], thickness_dimension
    )[0]
    extent = rate_col * jnp.exp(-energy / depth_temp)
    mass_ratio_after = residue + (mass_ratio - residue) * jnp.exp(-extent)
    warmed_fields = (
        depth_temp - HEAT_OF_PYROLYSIS * (mass_ratio - mass_ratio_after) / mass_ratio_after
    )
    diffuse_thermal_energy = charred + (virgin - charred) * (mass_ratio_after - residue) / (
        1.0 - residue
    )
    return (warmed_fields, mass_ratio_after, diffuse_thermal_energy)


def solve_x(pieces):
    return solve_lines(pieces, float(R_X), 0)


def sweep_trailing_lines(pieces):
    return solve_lines(pieces, float(R_Y), 1)


def per_device(
    kelvin_start,
    mass_ratio,
    material_region_labels,
    pristine_conductivity,
    burnt_conductivity,
    burnt_mass_ratio,
    arrhenius_prefactor,
    onset_kelvin,
    exchange_film_strength,
    stagnation_kelvin,
    receiving_element,
    occupied_slot_totals,
):
    patch_leading_extent, patch_trailing_extent, layer_number = kelvin_start.shape
    sources = lax.axis_size("row")
    cell_count = patch_leading_extent * patch_trailing_extent
    slot_index = jnp.arange(exchange_film_strength.shape[-1], dtype=jnp.int32)
    live_slots = (slot_index < occupied_slot_totals[..., None]).astype(jnp.float32)
    blending_shares = (exchange_film_strength * live_slots)[0, 0]
    flux_arriving = blending_shares * stagnation_kelvin[0, 0]
    targets = receiving_element[0, 0]
    offsets = jnp.arange(sources, dtype=jnp.int32)[:, None] * cell_count + targets
    flat_ids = offsets.reshape(-1)
    tile_weight = jax.ops.segment_sum(
        blending_shares.reshape(-1), flat_ids, num_segments=sources * cell_count
    )
    tile_heat = jax.ops.segment_sum(
        flux_arriving.reshape(-1), flat_ids, num_segments=sources * cell_count
    )
    exterior_multiplier, exterior_flux_amount = (
        lax.psum_scatter(tile_weight, "row", scatter_dimension=0, tiled=True),
        lax.psum_scatter(tile_heat, "row", scatter_dimension=0, tiled=True),
    )
    exterior_multiplier = exterior_multiplier.reshape(patch_leading_extent, patch_trailing_extent)
    exterior_flux_amount = exterior_flux_amount.reshape(patch_leading_extent, patch_trailing_extent)
    property_arrays = (
        pristine_conductivity,
        burnt_conductivity,
        burnt_mass_ratio,
        arrhenius_prefactor,
        onset_kelvin,
    )
    warmed_fields, mass_ratio_after, diffuse_thermal_energy = decompose_through_layers(
        kelvin_start,
        mass_ratio,
        material_region_labels,
        property_arrays,
        exterior_multiplier,
        exterior_flux_amount,
    )
    forcing_vector = mass_ratio_after * warmed_fields
    line_share = patch_trailing_extent * layer_number // sources
    flat_parts = (forcing_vector, mass_ratio_after, diffuse_thermal_energy)
    solved_x = solve_x(
        (
            lax.all_to_all(flat_parts[0], "row", split_axis=1, concat_axis=0, tiled=True),
            lax.all_to_all(flat_parts[1], "row", split_axis=1, concat_axis=0, tiled=True),
            lax.all_to_all(flat_parts[2], "row", split_axis=1, concat_axis=0, tiled=True),
        )
    )
    across = lax.all_to_all(solved_x, "row", split_axis=0, concat_axis=1, tiled=True)
    forcing_vector_other = mass_ratio_after * across
    solved_state = sweep_trailing_lines(
        (
            lax.all_to_all(forcing_vector_other, "col", split_axis=0, concat_axis=1, tiled=True),
            lax.all_to_all(mass_ratio_after, "col", split_axis=0, concat_axis=1, tiled=True),
            lax.all_to_all(diffuse_thermal_energy, "col", split_axis=0, concat_axis=1, tiled=True),
        )
    )
    kelvin_after = lax.all_to_all(solved_state, "col", split_axis=1, concat_axis=0, tiled=True)
    return (kelvin_after, mass_ratio_after)


def solution(mesh):
    return jax.shard_map(
        per_device,
        mesh=mesh,
        in_specs=(
            P("row", "col", None),
            P("row", "col", None),
            P("row", "col"),
            P(),
            P(),
            P(),
            P(),
            P(),
            P("row", "col", None, None),
            P("row", "col", None, None),
            P("row", "col", None, None),
            P("row", "col", None),
        ),
        out_specs=(P("row", "col", None), P("row", "col", None)),
        check_vma=False,
    )
```

profile of v0, /device:TPU:1, one launch (start us, length us, event | category | flops | bytes accessed | tf_op | source)
XLA Modules:
  0.0 658.0 jit_solution(1565937443796117026)
XLA Ops:
  8.8 57.7 %scatter_custom_fusion = f32[32768]{0:T(1024)} fusion(s32[8192]{0:T(1024)S(1)} %bitcast.253, f32[8192]{0:T(1024)S(1)} %get-tuple-element.52, f32[]{:T(128)} %constant.67.clone.1), kind=kCustom, calls=%fused_computation.156 | custom fusion | flops 8192 | bytes 131076 | tf_op jit(solution)/shard_map/scatter-add | solution.py:187
  66.5 57.6 %scatter_custom_fusion.1 = f32[32768]{0:T(1024)} fusion(s32[8192]{0:T(1024)S(1)} %bitcast.254, f32[8192]{0:T(1024)S(1)} %get-tuple-element.53, f32[]{:T(128)} %constant.67.clone.1), kind=kCustom, calls=%fused_computation.154 | custom fusion | flops 8192 | bytes 131076 | tf_op jit(solution)/shard_map/scatter-add | solution.py:184
  125.6 4.5 slice.1033
  130.1 4.5 slice.1025
  134.7 4.5 slice.1020
  139.2 4.5 slice.1022
  143.7 1.3 dynamic-slice.16
  145.8 236.7 %all-reduce.121.cloned.1.call-done = (f32[32768]{0:T(1024)}, f32[32768]{0:T(1024)}) async-done(((f32[32768]{0:T(1024)}, f32[32768]{0:T(1024)}), (f32[32768]{0:T(1024)}, f32[32768]{0:T(1024)})) %all-reduce.121.cloned.1.call-update) | async-done | bytes 262160
  383.9 4.5 slice.1017
  388.4 4.5 slice.1021
  393.4 4.5 slice.1024
  397.9 4.5 slice.1032
  403.0 2.3 slice.1028
  405.3 3.0 slice.1030
  408.3 2.3 slice.1035
  410.6 3.0 slice.1044
  413.6 2.3 slice.1029
  415.9 3.0 slice.1031
  418.9 2.3 slice.1045
  421.2 3.0 slice.1037
  424.2 1.7 multiply_add_fusion.10
  425.9 1.6 slice.1040
  427.5 1.9 slice.1042
  429.5 1.8 slice.1047
  431.3 1.9 slice.1056
  433.2 1.8 slice.1041
  435.0 1.9 slice.1043
  437.0 1.8 slice.1057
  438.8 1.9 slice.1049
  440.7 2.5 multiply_add_fusion.8
  443.2 1.3 slice.1052
  444.5 1.4 slice.1054
  445.9 1.3 slice.1059
  447.2 1.4 slice.1068
  448.5 1.3 slice.1053
  449.8 1.4 slice.1055
  451.2 1.3 slice.1069
  452.5 1.4 slice.1061
  453.9 2.7 multiply_add_fusion.6
  465.1 2.5 multiply_add_fusion.4
  474.1 1.8 fusion.222
  477.4 1.9 divide_bitcast_fusion.5
  479.3 1.1 copy.514
  481.3 2.1 divide_bitcast_fusion.4
  485.5 1.9 divide_bitcast_fusion.3
  495.9 8.0 %all-to-all-start = ((f32[8,64,128]{2,0,1:T(8,128)}), f32[8,64,128]{2,0,1:T(8,128)S(1)}, u32[]{:S(2)}, u32[]{:S(2)}) async-start(f32[8,64,128]{2,0,1:T(8,128)} %copy.540), calls=%async_computation | async-start | bytes 524288 | tf_op jit(solution)/shard_map/all_to_all | solution.py:216
  503.9 2.0 divide_add_fusion
  505.9 1.8 copy.541
  507.7 11.8 %all-to-all-done = f32[8,64,128]{2,0,1:T(8,128)S(1)} async-done(((f32[8,64,128]{2,0,1:T(8,128)}), f32[8,64,128]{2,0,1:T(8,128)S(1)}, u32[]{:S(2)}, u32[]{:S(2)}) %all-to-all-start) | async-done | bytes 262176 | tf_op jit(solution)/shard_map/all_to_all | solution.py:216
  519.5 6.2 all-to-all-start.1
  525.7 1.8 copy.542
  527.5 13.6 %all-to-all-done.1 = f32[8,64,128]{2,0,1:T(8,128)S(1)} async-done(((f32[8,64,128]{2,0,1:T(8,128)}), f32[8,64,128]{2,0,1:T(8,128)S(1)}, u32[]{:S(2)}, u32[]{:S(2)}) %all-to-all-start.1) | async-done | bytes 262176 | tf_op jit(solution)/shard_map/all_to_all | solution.py:218
  541.2 6.4 all-to-all-start.2
  547.8 15.2 %all-to-all-done.2 = f32[8,64,128]{2,0,1:T(8,128)S(1)} async-done(((f32[8,64,128]{2,0,1:T(8,128)}), f32[8,64,128]{2,0,1:T(8,128)S(1)}, u32[]{:S(2)}, u32[]{:S(2)}) %all-to-all-start.2) | async-done | bytes 262176 | tf_op jit(solution)/shard_map/all_to_all | solution.py:217
  563.0 19.4 %all-to-all-start.5 = ((f32[8,64,128]{2,1,0:T(8,128)}), f32[8,64,128]{2,1,0:T(8,128)S(1)}, u32[]{:S(2)}, u32[]{:S(2)}) async-start(f32[8,64,128]{2,1,0:T(8,128)} %divide_add_fusion), calls=%async_computation.5 | async-start | bytes 524288 | tf_op jit(solution)/shard_map/all_to_all | solution.py:227
  585.9 3.0 all-to-all-done.5
  588.9 6.3 all-to-all-start.3
  595.3 18.6 %all-to-all-done.3 = f32[512,1,128]{2,1,0:T(1,128)S(1)} async-done(((f32[512,1,128]{2,1,0:T(1,128)}), f32[512,1,128]{2,1,0:T(1,128)S(1)}, u32[]{:S(2)}, u32[]{:S(2)}) %all-to-all-start.3) | async-done | bytes 262176 | tf_op jit(solution)/shard_map/all_to_all | solution.py:221
  613.9 6.7 %all-to-all-start.6 = ((f32[8,64,128]{2,1,0:T(8,128)}), f32[8,64,128]{2,1,0:T(8,128)S(1)}, u32[]{:S(2)}, u32[]{:S(2)}) async-start(f32[8,64,128]{2,1,0:T(8,128)} %get-tuple-element.163), calls=%async_computation.6 | async-start | bytes 524288 | tf_op jit(solution)/shard_map/all_to_all | solution.py:226
  620.5 1.7 bitcast_multiply_fusion
  622.3 4.8 all-to-all-done.6
  627.1 4.4 all-to-all-start.4
  632.1 5.9 all-to-all-done.4
  640.3 9.9 %all_to_all.120 = f32[1,512,128]{2,0,1:T(1,128)S(1)} all-to-all(f32[1,512,128]{2,0,1:T(1,128)S(1)} %bitcast.222), channel_id=1, replica_groups=mesh['row'=64,'col'=8] {'col'}, dimensions={1} | all-to-all | bytes 524288 | tf_op jit(solution)/shard_map/all_to_all | solution.py:230
  (323 shorter events, 39.5 us)
Async XLA Ops:
  7.2 0.8 copy-start.16
  7.2 375.3 %all-reduce.121.cloned.1.call-start = ((), (), s32[]{:S(2)}) async-start(), calls=%async_computation.8 | async-start | bytes 524288
  7.9 0.8 copy-start.17
  7.9 0.8 copy-start.18
  8.0 0.7 copy-start.20
  8.8 116.2 %copy-start.11 = (f32[8,64,128]{2,1,0:T(8,128)S(1)}, f32[8,64,128]{2,1,0:T(8,128)}, u32[]{:S(2)}) copy-start(f32[8,64,128]{2,1,0:T(8,128)} %param.17) | copy-start | bytes 786436
  8.8 116.2 %copy-start.15 = (f32[8,64,128]{2,1,0:T(8,128)S(1)}, f32[8,64,128]{2,1,0:T(8,128)}, u32[]{:S(2)}) copy-start(f32[8,64,128]{2,1,0:T(8,128)} %param.16) | copy-start | bytes 786436
  124.1 0.7 copy-start.19
  124.1 0.7 copy-start.21
  124.1 0.7 copy-start.22
  124.1 0.7 copy-start.23
  124.1 0.7 copy-start.24
  124.1 0.7 copy-start.25
  472.9 1.1 copy-start.9
  476.4 1.0 copy-start.10
  479.3 2.0 copy-start.7
  479.3 2.0 copy-start.8
  481.3 4.1 copy-start.5
  481.3 4.1 copy-start.6
  483.4 2.0 copy-start.3
  483.4 2.0 copy-start.4
  487.3 0.9 copy-start.13
  488.3 1.0 copy-start.1
  488.3 1.0 copy-start.2
  488.5 1.0 copy-start
  490.4 0.9 copy-start.14
  493.1 1.0 copy-start.12
  495.9 23.6 %all-to-all-start = ((f32[8,64,128]{2,0,1:T(8,128)}), f32[8,64,128]{2,0,1:T(8,128)S(1)}, u32[]{:S(2)}, u32[]{:S(2)}) async-start(f32[8,64,128]{2,0,1:T(8,128)} %copy.540), calls=%async_computation | async-start | bytes 524288 | tf_op jit(solution)/shard_map/all_to_all | solution.py:216
  519.5 21.7 %all-to-all-start.1 = ((f32[8,64,128]{2,0,1:T(8,128)}), f32[8,64,128]{2,0,1:T(8,128)S(1)}, u32[]{:S(2)}, u32[]{:S(2)}) async-start(f32[8,64,128]{2,0,1:T(8,128)} %copy.541), calls=%async_computation.1 | async-start | bytes 524288 | tf_op jit(solution)/shard_map/all_to_all | solution.py:218
  541.2 21.8 %all-to-all-start.2 = ((f32[8,64,128]{2,0,1:T(8,128)}), f32[8,64,128]{2,0,1:T(8,128)S(1)}, u32[]{:S(2)}, u32[]{:S(2)}) async-start(f32[8,64,128]{2,0,1:T(8,128)} %copy.542), calls=%async_computation.2 | async-start | bytes 524288 | tf_op jit(solution)/shard_map/all_to_all | solution.py:217
  563.0 25.9 %all-to-all-start.5 = ((f32[8,64,128]{2,1,0:T(8,128)}), f32[8,64,128]{2,1,0:T(8,128)S(1)}, u32[]{:S(2)}, u32[]{:S(2)}) async-start(f32[8,64,128]{2,1,0:T(8,128)} %divide_add_fusion), calls=%async_computation.5 | async-start | bytes 524288 | tf_op jit(solution)/shard_map/all_to_all | solution.py:227
  588.9 25.0 %all-to-all-start.3 = ((f32[512,1,128]{2,1,0:T(1,128)}), f32[512,1,128]{2,1,0:T(1,128)S(1)}, u32[]{:S(2)}, u32[]{:S(2)}) async-start(f32[512,1,128]{2,1,0:T(1,128)} %bitcast.85), calls=%async_computation.3 | async-start | bytes 524288 | tf_op jit(solution)/shard_map/all_to_all | solution.py:221
  613.9 13.2 %all-to-all-start.6 = ((f32[8,64,128]{2,1,0:T(8,128)}), f32[8,64,128]{2,1,0:T(8,128)S(1)}, u32[]{:S(2)}, u32[]{:S(2)}) async-start(f32[8,64,128]{2,1,0:T(8,128)} %get-tuple-element.163), calls=%async_computation.6 | async-start | bytes 524288 | tf_op jit(solution)/shard_map/all_to_all | solution.py:226
  627.1 10.9 %all-to-all-start.4 = ((f32[8,64,128]{2,1,0:T(8,128)}), f32[8,64,128]{2,1,0:T(8,128)S(1)}, u32[]{:S(2)}, u32[]{:S(2)}) async-start(f32[8,64,128]{2,1,0:T(8,128)} %bitcast_multiply_fusion), calls=%async_computation.4 | async-start | bytes 524288 | tf_op jit(solution)/shard_map/all_to_all | solution.py:225
Sparse Core Ops, SparseCore 0:
  124.3 258.1 all-reduce.120
where the time goes:
time: 667 us; the launch traced here: 658 us
  waiting for transfers between devices  310 us (46%)
  other arithmetic  142 us (21%)
  local copies, waits for them, and re-layouts  122 us (18%)
  starting transfers between devices  57.4 us (9%)
  between operations  16.5 us (2%)
  blocking collectives  9.95 us (1%)
    unnamed x2, waiting for transfers between devices  237 us
    slice x177, local copies, waits for them, and re-layouts, take_part(): return lax.slice_in_dim(values, first_index, end_index, stride, solve_dim)  101 us
    scatter-add x1, other arithmetic, per_device(): jax.ops.segment_sum(flux_arriving.reshape(-1), flat_ids, num_segments=sou...  57.7 us
    scatter-add x1, other arithmetic, per_device(): jax.ops.segment_sum(blending_shares.reshape(-1), flat_ids, num_segments=s...  57.6 us
    all_to_all x1, starting transfers between devices, per_device(): lax.all_to_all(diffuse_thermal_energy, 'col', split_axis=0, concat_axis=1...  19.4 us
    all_to_all x1, waiting for transfers between devices, per_device(): lax.all_to_all(solved_x, 'row', split_axis=0, concat_axis=1, tiled=True)  18.6 us
    all_to_all x1, waiting for transfers between devices, per_device(): lax.all_to_all(flat_parts[1], 'row', split_axis=1, concat_axis=0, tiled=T...  15.2 us
    all_to_all x1, waiting for transfers between devices, per_device(): lax.all_to_all(flat_parts[2], 'row', split_axis=1, concat_axis=0, tiled=T...  13.6 us
  transfers between devices with their start and end apart: 8, of which 8 were waited for; matrix products, arithmetic and copies ran while one was open for 5% of the time, Pallas kernels for 0%

commit v1 on v0

v1 whole, which is shorter than its diff:
```python
import functools

import jax
import jax.numpy as jnp
from jax import lax
from jax.experimental import pallas as pl
from jax.experimental.pallas import tpu as pltpu
from jax.sharding import PartitionSpec as P

R_X = 32.0
R_Y = 64.0
R_Z = 1024.0
EXTERIOR_SHARE = 16.0
HEAT_OF_PYROLYSIS = 0.3

MESH = pl.DeviceIdType.MESH
F32 = jnp.float32
BF16 = jnp.bfloat16

FACE_ROWS = 3
PORT_ROWS = 5
BACK_ROWS = 2
DEPTH_ROWS = 64


def kernel(
    n_row, n_col, cx, cy, depth,
    kel_h, mass_h, lab_h, virgin_h, charred_h, residue_h, rate_h, energy_h,
    film_h, stag_h, elem_h, count_h,
    out_h, mass_out_h,
    kel, mass, lab, virgin_s, charred_s, residue_s, rate_s, energy_s,
    film, stag, elem, count,
    props, sol_u, sol_v, first_u, first_v,
    face_s, face_r, split, cond, mass2, rhs,
    k_row_s, k_row_r, k_col_s, k_col_r,
    gx, lx, px, port_s, port_r, back_s, back_r,
    gy, dy, qy, ry, py, ypt_s, ypt_r, yrh_s, yrh_r, yfac, ysol, out,
    in_sem, out_sem, send_sem, recv_sem,
):
    row, col = lax.axis_index("row"), lax.axis_index("col")

    loads = [
        (film_h, film), (stag_h, stag), (elem_h, elem), (count_h, count),
        (kel_h, kel), (mass_h, mass), (lab_h, lab),
        (virgin_h, virgin_s), (charred_h, charred_s), (residue_h, residue_s),
        (rate_h, rate_s), (energy_h, energy_s),
    ]
    loads = [pltpu.make_async_copy(a, b, in_sem.at[i]) for i, (a, b) in enumerate(loads)]
    for load in loads:
        load.start()

    barrier = pltpu.get_barrier_semaphore()

    def greet_row(t, _):
        pl.semaphore_signal(
            barrier, inc=1, device_id={"row": lax.rem(row + t, n_row)}, device_id_type=MESH
        )
        return 0

    def greet_col(t, _):
        pl.semaphore_signal(
            barrier, inc=1, device_id={"col": lax.rem(col + t, n_col)}, device_id_type=MESH
        )
        return 0

    lax.fori_loop(1, n_row, greet_row, 0)
    lax.fori_loop(1, n_col, greet_col, 0)

    lane = lax.broadcasted_iota(jnp.int32, (cy, depth), 1)

    def strided(ref, value):
        return ref.at[pl.ds(value, ref.shape[0] // 8, stride=8), :]

    def slot(ref, index, rows):
        return ref.at[pl.ds(pl.multiple_of(index * 8, 8), rows), :]

    def exchange_row(source, target, rows, phase):
        def send(t, _):
            peer = lax.rem(row + t, n_row)
            pltpu.make_async_remote_copy(
                src_ref=slot(source, peer, rows),
                dst_ref=slot(target, row, rows),
                send_sem=send_sem.at[phase],
                recv_sem=recv_sem.at[phase],
                device_id={"row": peer},
                device_id_type=MESH,
            ).start()
            return 0

        lax.fori_loop(1, n_row, send, 0)
        slot(target, row, rows)[...] = slot(source, row, rows)[...]

    def row_bytes(ref, rows):
        return ref.at[pl.ds(0, (n_row - 1) * rows), :]

    def exchange_col(source, target, phase):
        def send(t, _):
            peer = lax.rem(col + t, n_col)
            pltpu.make_async_remote_copy(
                src_ref=source,
                dst_ref=target.at[col],
                send_sem=send_sem.at[phase],
                recv_sem=recv_sem.at[phase],
                device_id={"col": peer},
                device_id_type=MESH,
            ).start()
            return 0

        lax.fori_loop(1, n_col, send, 0)
        target[col] = source[...]

    def await_bytes(ref, sem):
        pltpu.make_async_copy(ref, ref, sem).wait()

    for load in loads[:4]:
        load.wait()
    counts = jnp.broadcast_to(count[...].astype(F32), (8, n_row)).T[:, 0:1]
    face_lane = lax.broadcasted_iota(jnp.int32, film.shape, 1).astype(F32)
    weight = jnp.where(face_lane < counts, film[...], 0.0)
    strided(face_s, 0)[...] = weight
    strided(face_s, 1)[...] = jnp.where(face_lane < counts, weight * stag[...], 0.0)
    strided(face_s, 2)[...] = elem[...].astype(F32)
    pl.semaphore_wait(barrier, n_row - 1 + n_col - 1)
    exchange_row(face_s, face_r, FACE_ROWS, 0)

    for load in loads[4:]:
        load.wait()
    zone = lab[...]

    def look_up(table):
        value = jnp.full(zone.shape, table[0], F32)
        for z in range(1, 8):
            value = jnp.where(zone == z, table[z], value)
        return value

    virgin, charred, residue = look_up(virgin_s), look_up(charred_s), look_up(residue_s)
    slope = (virgin - charred) / (1.0 - residue)
    table = jnp.concatenate(
        [charred, slope, residue, look_up(rate_s), look_up(energy_s)], axis=0
    ).T
    for p in range(5):
        for x in range(cx):
            props[p, x * cy : (x + 1) * cy, :] = jnp.broadcast_to(
                table[:, p * cx + x : p * cx + x + 1], (cy, depth)
            )

    def depth_sweep(x, _):
        rows = pl.ds(pl.multiple_of(x * cy, cy), cy)
        m = mass[rows, :]
        k = props[0, rows, :] + props[1, rows, :] * (m - props[2, rows, :])
        a = jnp.where(lane == 0, 0.0, (-0.5 * R_Z) * (pltpu.roll(k, 1, 1) + k))
        d = m - a - pltpu.roll(a, depth - 1, 1)
        b = m * kel[rows, :]
        e = jnp.where(lane == 0, 1.0, 0.0)
        step = 1
        while step < depth:
            inv = 1.0 / d
            h = a * inv
            back = depth - step
            al = a * pltpu.roll(inv, step, 1)
            d = d - al * a - pltpu.roll(a * h, back, 1)
            b = b - al * pltpu.roll(b, step, 1) - pltpu.roll(h * b, back, 1)
            e = e - al * pltpu.roll(e, step, 1) - pltpu.roll(h * e, back, 1)
            a = -al * pltpu.roll(a, step, 1)
            step *= 2
        inv = 1.0 / d
        u, v = b * inv, e * inv
        sol_u[rows, :] = u
        sol_v[rows, :] = v
        first_u[...] = jnp.where(lane == x, u[:, 0:1], first_u[...])
        first_v[...] = jnp.where(lane == x, v[:, 0:1], first_v[...])
        return 0

    first_u[...] = jnp.zeros(first_u.shape, F32)
    first_v[...] = jnp.zeros(first_v.shape, F32)
    lax.fori_loop(0, cx, depth_sweep, 0)

    await_bytes(row_bytes(face_r, FACE_ROWS), recv_sem.at[0])
    for j in range(2):
        value = strided(face_r, j)[...]
        high = value.astype(BF16).astype(F32)
        split[j] = high
        split[2 + j] = value - high
    place = strided(face_r, 2)[...]
    place_x = jnp.floor(place * (1.0 / cy))
    split[4] = place_x
    split[5] = place - place_x * cy
    slots = film.shape[1]
    x_index = lax.broadcasted_iota(jnp.int32, (cx, slots), 0).astype(F32)
    y_index = lax.broadcasted_iota(jnp.int32, (cy, slots), 0).astype(F32)

    def add_faces(pair, total):
        lefts, rights = [], []
        for half in range(2):
            src = pair * 2 + half
            in_x = x_index == split[4, pl.ds(src, 1), :]
            lefts.append(
                jnp.concatenate(
                    [jnp.where(in_x, split[j, pl.ds(src, 1), :], 0.0) for j in range(4)], axis=0
                )
            )
            rights.append(jnp.where(y_index == split[5, pl.ds(src, 1), :], 1.0, 0.0))
        left = jnp.concatenate(lefts, axis=1).astype(BF16)
        right = jnp.concatenate(rights, axis=1).astype(BF16)
        return total + lax.dot_general(
            right, left, (((1,), (1,)), ((), ())), preferred_element_type=F32
        )

    sums = lax.fori_loop(0, n_row // 2, add_faces, jnp.zeros((cy, 4 * cx), F32), unroll=True)
    wall_w = sums[:, 0:cx] + sums[:, 2 * cx : 3 * cx]
    wall_q = sums[:, cx : 2 * cx] + sums[:, 3 * cx : 4 * cx]
    alpha = (
        EXTERIOR_SHARE
        * (wall_q - wall_w * first_u[:, 0:cx])
        / (1.0 + EXTERIOR_SHARE * wall_w * first_v[:, 0:cx])
    )

    def send_k(source, target, axis, position, size, phase):
        copy = pltpu.make_async_remote_copy(
            src_ref=source,
            dst_ref=target,
            send_sem=send_sem.at[phase],
            recv_sem=recv_sem.at[phase],
            device_id={axis: lax.rem(position + size - 1, size)},
            device_id_type=MESH,
        )
        copy.start()
        return copy

    for x in range(cx):
        rows = pl.ds(x * cy, cy)
        m = mass[rows, :]
        res = props[2, rows, :]
        t = sol_u[rows, :] + alpha[:, x : x + 1] * sol_v[rows, :]
        extent = props[3, rows, :] * jnp.exp(-props[4, rows, :] / t)
        excess = (m - res) * jnp.exp(-extent)
        m2 = res + excess
        mass2[rows, :] = m2
        rhs[rows, :] = m2 * t - HEAT_OF_PYROLYSIS * (m - m2)
        cond[rows, :] = props[0, rows, :] + props[1, rows, :] * excess
        if x == 0:
            k_row_s[...] = cond[rows, :]
            k_row = send_k(k_row_s, k_row_r, "row", row, n_row, 1)
    mass_out = pltpu.make_async_copy(mass2, mass_out_h, out_sem.at[0])
    mass_out.start()
    k_col_s[...] = cond[pl.ds(0, cx, stride=cy), :]
    k_col = send_k(k_col_s, k_col_r, "col", col, n_col, 2)

    def plane(ref, x):
        return ref[pl.ds(x * cy, cy), :]

    face = (0.5 * R_X) * (plane(cond, 0) + plane(cond, 1))
    left = plane(mass2, 0) + face
    left_rhs = plane(rhs, 0)
    coupling, held, right_hand = face, face, plane(rhs, 1)
    for x in range(1, cx):
        if x < cx - 1:
            face = (0.5 * R_X) * (plane(cond, x) + plane(cond, x + 1))
        else:
            k_row.wait_recv()
            face = (0.5 * R_X) * (plane(cond, x) + k_row_r[...])
            face = jnp.where(row == n_row - 1, 0.0, face)
        inv = 1.0 / (plane(mass2, x) + held + face)
        g, l, p = face * inv, coupling * inv, right_hand * inv
        gx[x], lx[x], px[x] = g, l, p
        left = left - coupling * l
        left_rhs = left_rhs + coupling * p
        coupling = coupling * g
        held = face - face * g
        if x < cx - 1:
            right_hand = plane(rhs, x + 1) + right_hand * g
        else:
            right_hand = right_hand * g
    for j, value in enumerate((left, -coupling, held, left_rhs, right_hand)):
        strided(port_s, j)[...] = value
    exchange_row(port_s, port_r, PORT_ROWS, 3)

    k_col.wait_recv()

    def line(ref, y):
        return ref[pl.ds(y, cx, stride=cy), :]

    k_first = k_col_r[...]
    face0 = (0.5 * R_Y) * (line(cond, 0) + line(cond, 1))

    def port_y(y, carry):
        left, coupling, held, k_here = carry
        after = lax.rem(y + 1, cy)
        k_next = jnp.where(after == 0, k_first, line(cond, after))
        face = (0.5 * R_Y) * (k_here + k_next)
        face = jnp.where((after == 0) & (col == n_col - 1), 0.0, face)
        inv = 1.0 / (line(mass2, y) + held + face)
        g, l = face * inv, coupling * inv
        gy[y], dy[y], qy[y] = g, inv, l
        return left - coupling * l, coupling * g, face - face * g, k_next

    left, coupling, held, _ = lax.fori_loop(
        1, cy, port_y, (line(mass2, 0) + face0, face0, face0, line(cond, 1)), unroll=7
    )
    ypt_s[0], ypt_s[1], ypt_s[2] = left, -coupling, held
    exchange_col(ypt_s, ypt_r, 4)

    await_bytes(row_bytes(port_r, PORT_ROWS), recv_sem.at[3])
    down = strided(port_r, 1)[...]
    a = pltpu.roll(down, 1, 0)
    d = strided(port_r, 0)[...] + pltpu.roll(strided(port_r, 2)[...], 1, 0)
    b = strided(port_r, 3)[...] + pltpu.roll(strided(port_r, 4)[...], 1, 0)
    step = 1
    while step < n_row:
        inv = 1.0 / d
        h = a * inv
        back = n_row - step
        al = a * pltpu.roll(inv, step, 0)
        d = d - al * a - pltpu.roll(a * h, back, 0)
        b = b - al * pltpu.roll(b, step, 0) - pltpu.roll(h * b, back, 0)
        a = -al * pltpu.roll(a, step, 0)
        step *= 2
    first = b / d
    strided(back_s, 0)[...] = first
    strided(back_s, 1)[...] = pltpu.roll(first, n_row - 1, 0)
    exchange_row(back_s, back_r, BACK_ROWS, 5)

    def answer_y(i, carry):
        q, r = carry
        y = cy - 1 - i
        g = gy[y]
        q, r = qy[y] + g * q, g * r
        qy[y], ry[y] = q, r
        return q, r

    zero = jnp.zeros((cx, depth), F32)
    lax.fori_loop(0, cy - 1, answer_y, (zero, zero + 1.0), unroll=7)
    qy[0], ry[0] = zero + 1.0, zero

    await_bytes(ypt_r.at[pl.ds(0, n_col - 1)], recv_sem.at[4])
    diag = ypt_r[0, 0]
    for i in range(n_col):
        inv = 1.0 / diag
        yfac[0, i] = inv
        if i < n_col - 1:
            off = ypt_r[i, 1]
            yfac[1, i] = off * inv
            diag = ypt_r[i + 1, 0] + ypt_r[i, 2] - off * off * inv

    await_bytes(row_bytes(back_r, BACK_ROWS), recv_sem.at[5])
    x_first, x_next = strided(back_r, 0)[...], strided(back_r, 1)[...]
    rhs[pl.ds(0, cy), :] = x_first * plane(mass2, 0)
    for x in range(cx - 1, 0, -1):
        x_next = px[x] + gx[x] * x_next + lx[x] * x_first
        rhs[pl.ds(x * cy, cy), :] = x_next * plane(mass2, x)

    def gather_rhs(y, carry):
        value = line(rhs, y)
        return carry[0] + qy[y] * value, carry[1] + ry[y] * value

    total = lax.fori_loop(0, cy, gather_rhs, (zero, zero), unroll=8)
    yrh_s[0], yrh_s[1] = total
    exchange_col(yrh_s, yrh_r, 6)

    def forward_y(y, carry):
        carry = line(rhs, y) + gy[y - 1] * carry
        py[y] = carry
        return carry

    def backward_y(i, carry):
        y = cy - 1 - i
        carry = py[y] * dy[y] + gy[y] * carry
        py[y] = carry
        return carry

    gy[0] = zero
    lax.fori_loop(1, cy, forward_y, zero, unroll=7)
    lax.fori_loop(0, cy - 1, backward_y, zero, unroll=7)
    py[0] = zero

    await_bytes(yrh_r.at[pl.ds(0, n_col - 1)], recv_sem.at[6])
    value = yrh_r[0, 0]
    ysol[0] = value
    for i in range(1, n_col):
        value = yrh_r[i, 0] + yrh_r[i - 1, 1] - yfac[1, i - 1] * value
        ysol[i] = value
    value = value * yfac[0, n_col - 1]
    ysol[n_col - 1] = value
    ysol[n_col] = zero
    for i in range(n_col - 2, -1, -1):
        value = ysol[i] * yfac[0, i] - yfac[1, i] * value
        ysol[i] = value
    y_first, y_next = ysol[col], ysol[col + 1]

    def finish(y, _):
        out[pl.ds(y, cx, stride=cy), :] = py[y] + qy[y] * y_first + ry[y] * y_next
        return 0

    lax.fori_loop(0, cy, finish, 0, unroll=8)
    result = pltpu.make_async_copy(out, out_h, out_sem.at[1])
    result.start()

    await_bytes(row_bytes(face_s, FACE_ROWS), send_sem.at[0])
    k_row.wait_send()
    k_col.wait_send()
    await_bytes(row_bytes(port_s, PORT_ROWS), send_sem.at[3])
    await_bytes(ypt_r.at[pl.ds(0, n_col - 1)], send_sem.at[4])
    await_bytes(row_bytes(back_s, BACK_ROWS), send_sem.at[5])
    await_bytes(yrh_r.at[pl.ds(0, n_col - 1)], send_sem.at[6])
    mass_out.wait()
    result.wait()


def per_device(n_row, n_col, kelvin, mass, labels, virgin, charred, residue, rate, energy, film, stag, elem, count):
    cx, cy, depth = kelvin.shape
    slots = film.shape[-1]
    cells = cx * cy
    vmem = lambda *shape: pltpu.VMEM(shape, F32)
    zones = virgin.shape[0]
    scratch = [
        vmem(cells, depth), vmem(cells, depth), pltpu.VMEM((cx, cy), jnp.int32),
        *[pltpu.SMEM((zones,), F32)] * 5,
        vmem(n_row, slots), vmem(n_row, slots), pltpu.VMEM((n_row, slots), jnp.int32),
        pltpu.VMEM((1, n_row), jnp.int32),
        vmem(5, cells, depth), vmem(cells, depth), vmem(cells, depth), vmem(cy, depth), vmem(cy, depth),
        vmem(n_row * 8, slots), vmem(n_row * 8, slots), vmem(6, n_row, slots),
        vmem(cells, depth), vmem(cells, depth), vmem(cells, depth),
        vmem(cy, depth), vmem(cy, depth), vmem(cx, depth), vmem(cx, depth),
        vmem(cx, cy, depth), vmem(cx, cy, depth), vmem(cx, cy, depth),
        *[vmem(n_row * 8, depth)] * 4,
        *[vmem(cy, cx, depth)] * 5,
        vmem(3, cx, depth), vmem(n_col, 3, cx, depth),
        vmem(2, cx, depth), vmem(n_col, 2, cx, depth),
        vmem(2, n_col, cx, depth), vmem(n_col + 1, cx, depth), vmem(cells, depth),
        pltpu.SemaphoreType.DMA((12,)), pltpu.SemaphoreType.DMA((2,)),
        pltpu.SemaphoreType.DMA((7,)), pltpu.SemaphoreType.DMA((7,)),
    ]
    whole = jax.ShapeDtypeStruct((cells, depth), F32)
    out, mass_out = pl.pallas_call(
        functools.partial(kernel, n_row, n_col, cx, cy, depth),
        out_shape=(whole, whole),
        in_specs=[pl.BlockSpec(memory_space=pl.ANY)] * 12,
        out_specs=(pl.BlockSpec(memory_space=pl.ANY),) * 2,
        scratch_shapes=scratch,
        compiler_params=pltpu.CompilerParams(
            collective_id=0, has_side_effects=True, vmem_limit_bytes=24 * 1024 * 1024
        ),
    )(
        kelvin.reshape(cells, depth), mass.reshape(cells, depth), labels,
        virgin, charred, residue, rate, energy,
        film.reshape(n_row, slots), stag.reshape(n_row, slots), elem.reshape(n_row, slots),
        count.reshape(1, n_row),
    )
    return out.reshape(kelvin.shape), mass_out.reshape(kelvin.shape)


def solution(mesh):
    field, surface, faces = P("row", "col", None), P("row", "col"), P("row", "col", None, None)
    return jax.shard_map(
        functools.partial(per_device, mesh.shape["row"], mesh.shape["col"]),
        mesh=mesh,
        in_specs=(field, field, surface, P(), P(), P(), P(), P(), faces, faces, faces, field),
        out_specs=(field, field),
        check_vma=False,
    )
```

time: 667 us -> 64.5 us (0.10); the launches traced: 658 us -> 64.1 us
  waiting for transfers between devices: 310 us -> 0 us
  other arithmetic: 142 us -> 0 us
  local copies, waits for them, and re-layouts: 122 us -> 6.27 us
  starting transfers between devices: 57.4 us -> 0 us
  Pallas kernels: 0 us -> 57.1 us
  between operations: 16.5 us -> 0.71 us
  blocking collectives: 9.95 us -> 0 us
    unnamed x2 -> x0, waiting for transfers between devices: 237 us -> none
    scatter-add x2 -> x0, other arithmetic: 115 us -> none  [the longest x1 57.7 us: per_device(): jax.ops.segment_sum(flux_arriving.reshape(-1), flat_ids, num_segments=sou...]
    slice x177 -> x0, local copies, waits for them, and re-layouts: 101 us -> none  [take_part(): return lax.slice_in_dim(values, first_index, end_index, stride, solve_dim)]
    all_to_all x7 -> x0, waiting for transfers between devices: 72.9 us -> none  [the longest x1 18.6 us: per_device(): lax.all_to_all(solved_x, 'row', split_axis=0, concat_axis=1, tiled=True)]
    all_to_all x7 -> x0, starting transfers between devices: 57.4 us -> none  [the longest x1 19.4 us: per_device(): lax.all_to_all(diffuse_thermal_energy, 'col', split_axis=0, concat_axis=1...]
    pallas_call x0 -> x1, Pallas kernels: none -> 57.1 us  [per_device(): pl.pallas_call(functools.partial(kernel, n_row, n_col, cx, cy, depth), ou...]
    add x19 -> x0, other arithmetic: 12.2 us -> none  [the longest x14 10.1 us: cyclic_solve(): odd_part + left_factor * left_part + right_factor * right_part]
    all_to_all x1 -> x0, blocking collectives: 9.95 us -> none  [per_device(): lax.all_to_all(solved_state, 'col', split_axis=1, concat_axis=0, tiled=True)]
  transfers between devices with their start and end apart: 8 -> 0, of which waited for: 8 -> 0; matrix products, arithmetic and copies ran while one was open for 5% -> 0% of each run, Pallas kernels for 0% -> 0%
where the time goes in v1:
time: 64.5 us; the launch traced here: 64.1 us
  Pallas kernels  57.1 us (89%)
  local copies, waits for them, and re-layouts  6.27 us (10%)
  between operations  0.71 us (1%)
    pallas_call x1, Pallas kernels, per_device(): pl.pallas_call(functools.partial(kernel, n_row, n_col, cx, cy, depth), ou...  57.1 us
    unnamed x26, local copies, waits for them, and re-layouts  6.27 us

profile of v1, /device:TPU:1, one launch (start us, length us, event | category | flops | bytes accessed | tf_op | source)
XLA Modules:
  0.0 64.1 jit_solution(9606286033441974486)
XLA Ops:
  0.6 0.0 copy-start.5
  0.6 0.0 copy-start.9
  0.7 0.0 copy-start.10
  0.7 0.0 copy-start.11
  0.7 0.0 copy-start.6
  0.7 0.0 copy-start.7
  0.7 0.0 copy-start.8
  0.7 0.6 copy-done.5
  1.3 0.0 copy-done.9
  1.3 0.0 copy-done.10
  1.3 0.0 copy-done.11
  1.3 0.0 copy-done.6
  1.4 0.0 copy-done.7
  1.4 0.0 copy-done.8
  1.4 0.0 copy-start
  1.4 0.9 %copy-done = f32[8,64,128]{2,1,0:T(8,128)S(1)} copy-done((f32[8,64,128]{2,1,0:T(8,128)S(1)}, f32[8,64,128]{2,1,0:T(8,128)}, u32[]{:S(2)}) %copy-start) | copy-done | bytes 262168
  2.3 0.0 copy-start.1
  2.3 0.9 %copy-done.1 = f32[8,64,128]{2,1,0:T(8,128)S(1)} copy-done((f32[8,64,128]{2,1,0:T(8,128)S(1)}, f32[8,64,128]{2,1,0:T(8,128)}, u32[]{:S(2)}) %copy-start.1) | copy-done | bytes 262168
  3.3 0.0 copy-start.2
  3.3 0.8 %copy-done.2 = f32[1,1,64,128]{3,2,1,0:T(8,128)S(1)} copy-done((f32[1,1,64,128]{3,2,1,0:T(8,128)S(1)}, f32[1,1,64,128]{3,2,1,0:T(8,128)}, u32[]{:S(2)}) %copy-start.2) | copy-done | bytes 32792
  4.0 0.0 copy-start.3
  4.0 0.8 %copy-done.3 = f32[1,1,64,128]{3,2,1,0:T(8,128)S(1)} copy-done((f32[1,1,64,128]{3,2,1,0:T(8,128)S(1)}, f32[1,1,64,128]{3,2,1,0:T(8,128)}, u32[]{:S(2)}) %copy-start.3) | copy-done | bytes 32792
  4.8 0.0 copy-start.4
  4.8 0.8 %copy-done.4 = s32[1,1,64,128]{3,2,1,0:T(8,128)S(1)} copy-done((s32[1,1,64,128]{3,2,1,0:T(8,128)S(1)}, s32[1,1,64,128]{3,2,1,0:T(8,128)}, u32[]{:S(2)}) %copy-start.4) | copy-done | bytes 32792
  5.6 57.1 %shard_map.131 = (f32[512,128]{1,0:T(8,128)S(1)}, f32[512,128]{1,0:T(8,128)S(1)}) custom-call(f32[512,128]{1,0:T(8,128)S(1)} %bitcast.8, f32[512,128]{1,0:T(8,128)S(1)} %bitcast.9, s32[8,64]{1,0:T(8,128)S(1)} %copy-done.5, f32[8]{0:T(128)S(1)} %copy-done.6, f32[8]{0:T(128)S(1)} %copy-done.7, f32[8]{0:T(128)S(1)} %copy-done.8, f32[8]{0:T(128)S(1)} %copy-done.9, ...), custom_call_target="tpu_custom_call" | custom-call | tf_op jit(solution)/shard_map/pallas_call | solution.py:434
  62.7 0.7 %copy.16 = f32[8,64,128]{2,1,0:T(8,128)} copy(f32[8,64,128]{2,1,0:T(8,128)S(1)} %bitcast.11) | data formatting | bytes 524288
  63.4 0.7 %copy.17 = f32[8,64,128]{2,1,0:T(8,128)} copy(f32[8,64,128]{2,1,0:T(8,128)S(1)} %bitcast.10) | data formatting | bytes 524288
Async XLA Ops:
  0.6 0.7 %copy-start.5 = (s32[8,64]{1,0:T(8,128)S(1)}, s32[8,64]{1,0:T(8,128)}, u32[]{:S(2)}) copy-start(s32[8,64]{1,0:T(8,128)} %lab_h.1) | copy-start | bytes 6148
  0.6 0.7 %copy-start.9 = (f32[8]{0:T(128)S(1)}, f32[8]{0:T(128)}, u32[]{:S(2)}) copy-start(f32[8]{0:T(128)} %rate_h.1) | copy-start | bytes 100
  0.7 0.7 %copy-start.10 = (f32[8]{0:T(128)S(1)}, f32[8]{0:T(128)}, u32[]{:S(2)}) copy-start(f32[8]{0:T(128)} %energy_h.1) | copy-start | bytes 100
  0.7 0.7 %copy-start.11 = (s32[1,1,64]{2,1,0:T(1,128)S(1)}, s32[1,1,64]{2,1,0:T(1,128)}, u32[]{:S(2)}) copy-start(s32[1,1,64]{2,1,0:T(1,128)} %param.23) | copy-start | bytes 772
  0.7 0.7 %copy-start.6 = (f32[8]{0:T(128)S(1)}, f32[8]{0:T(128)}, u32[]{:S(2)}) copy-start(f32[8]{0:T(128)} %virgin_h.1) | copy-start | bytes 100
  0.7 0.7 %copy-start.7 = (f32[8]{0:T(128)S(1)}, f32[8]{0:T(128)}, u32[]{:S(2)}) copy-start(f32[8]{0:T(128)} %charred_h.1) | copy-start | bytes 100
  0.7 0.7 %copy-start.8 = (f32[8]{0:T(128)S(1)}, f32[8]{0:T(128)}, u32[]{:S(2)}) copy-start(f32[8]{0:T(128)} %residue_h.1) | copy-start | bytes 100
  1.4 0.9 %copy-start = (f32[8,64,128]{2,1,0:T(8,128)S(1)}, f32[8,64,128]{2,1,0:T(8,128)}, u32[]{:S(2)}) copy-start(f32[8,64,128]{2,1,0:T(8,128)} %param.12) | copy-start | bytes 786436
  2.3 0.9 %copy-start.1 = (f32[8,64,128]{2,1,0:T(8,128)S(1)}, f32[8,64,128]{2,1,0:T(8,128)}, u32[]{:S(2)}) copy-start(f32[8,64,128]{2,1,0:T(8,128)} %param.13) | copy-start | bytes 786436
  3.3 0.8 %copy-start.2 = (f32[1,1,64,128]{3,2,1,0:T(8,128)S(1)}, f32[1,1,64,128]{3,2,1,0:T(8,128)}, u32[]{:S(2)}) copy-start(f32[1,1,64,128]{3,2,1,0:T(8,128)} %param.20) | copy-start | bytes 98308
  4.0 0.8 %copy-start.3 = (f32[1,1,64,128]{3,2,1,0:T(8,128)S(1)}, f32[1,1,64,128]{3,2,1,0:T(8,128)}, u32[]{:S(2)}) copy-start(f32[1,1,64,128]{3,2,1,0:T(8,128)} %param.21) | copy-start | bytes 98308
  4.8 0.8 %copy-start.4 = (s32[1,1,64,128]{3,2,1,0:T(8,128)S(1)}, s32[1,1,64,128]{3,2,1,0:T(8,128)}, u32[]{:S(2)}) copy-start(s32[1,1,64,128]{3,2,1,0:T(8,128)} %param.22) | copy-start | bytes 98308

commit v2 on v1

--- a/solution.py
+++ b/solution.py
@@ -17,10 +17,10 @@
 F32 = jnp.float32
 BF16 = jnp.bfloat16
 
+N_X = 4
 FACE_ROWS = 3
 PORT_ROWS = 5
 BACK_ROWS = 2
-DEPTH_ROWS = 64
 
 
 def kernel(
@@ -51,10 +51,17 @@
 
     barrier = pltpu.get_barrier_semaphore()
 
-    def greet_row(t, _):
-        pl.semaphore_signal(
-            barrier, inc=1, device_id={"row": lax.rem(row + t, n_row)}, device_id_type=MESH
-        )
+    def far_first(n, size):
+        return lax.rem(size + size // 2 + (n + 1) // 2 * (1 - 2 * lax.rem(n, 2)), size)
+
+    n_z = n_row // N_X
+
+    def row_peer(n):
+        x = lax.rem(row // n_z + far_first(lax.rem(n, N_X), N_X), N_X)
+        return x * n_z + lax.rem(lax.rem(row, n_z) + far_first(n // N_X, n_z), n_z)
+
+    def greet_row(n, _):
+        pl.semaphore_signal(barrier, inc=1, device_id={"row": row_peer(n)}, device_id_type=MESH)
         return 0
 
     def greet_col(t, _):
@@ -63,7 +70,7 @@
         )
         return 0
 
-    lax.fori_loop(1, n_row, greet_row, 0)
+    lax.fori_loop(0, n_row - 1, greet_row, 0)
     lax.fori_loop(1, n_col, greet_col, 0)
 
     lane = lax.broadcasted_iota(jnp.int32, (cy, depth), 1)
@@ -75,8 +82,8 @@
         return ref.at[pl.ds(pl.multiple_of(index * 8, 8), rows), :]
 
     def exchange_row(source, target, rows, phase):
-        def send(t, _):
-            peer = lax.rem(row + t, n_row)
+        def send(n, _):
+            peer = row_peer(n)
             pltpu.make_async_remote_copy(
                 src_ref=slot(source, peer, rows),
                 dst_ref=slot(target, row, rows),
@@ -87,7 +94,7 @@
             ).start()
             return 0
 
-        lax.fori_loop(1, n_row, send, 0)
+        lax.fori_loop(0, n_row - 1, send, 0)
         slot(target, row, rows)[...] = slot(source, row, rows)[...]
 
     def row_bytes(ref, rows):
@@ -120,8 +127,6 @@
     strided(face_s, 0)[...] = weight
     strided(face_s, 1)[...] = jnp.where(face_lane < counts, weight * stag[...], 0.0)
     strided(face_s, 2)[...] = elem[...].astype(F32)
-    pl.semaphore_wait(barrier, n_row - 1 + n_col - 1)
-    exchange_row(face_s, face_r, FACE_ROWS, 0)
 
     for load in loads[4:]:
         load.wait()
@@ -175,6 +180,9 @@
     first_v[...] = jnp.zeros(first_v.shape, F32)
     lax.fori_loop(0, cx, depth_sweep, 0)
 
+    pl.semaphore_wait(barrier, n_row - 1 + n_col - 1)
+    exchange_row(face_s, face_r, FACE_ROWS, 0)
+
     await_bytes(row_bytes(face_r, FACE_ROWS), recv_sem.at[0])
     for j in range(2):
         value = strided(face_r, j)[...]
@@ -241,8 +249,6 @@
         if x == 0:
             k_row_s[...] = cond[rows, :]
             k_row = send_k(k_row_s, k_row_r, "row", row, n_row, 1)
-    mass_out = pltpu.make_async_copy(mass2, mass_out_h, out_sem.at[0])
-    mass_out.start()
     k_col_s[...] = cond[pl.ds(0, cx, stride=cy), :]
     k_col = send_k(k_col_s, k_col_r, "col", col, n_col, 2)
 
@@ -300,6 +306,9 @@
     ypt_s[0], ypt_s[1], ypt_s[2] = left, -coupling, held
     exchange_col(ypt_s, ypt_r, 4)
 
+    mass_out = pltpu.make_async_copy(mass2, mass_out_h, out_sem.at[0])
+    mass_out.start()
+
     await_bytes(row_bytes(port_r, PORT_ROWS), recv_sem.at[3])
     down = strided(port_r, 1)[...]
     a = pltpu.roll(down, 1, 0)
@@ -404,6 +413,14 @@
     await_bytes(yrh_r.at[pl.ds(0, n_col - 1)], send_sem.at[6])
     mass_out.wait()
     result.wait()
+
+
+def hand_over(a, b, a_out, b_out, sems):
+    copies = [pltpu.make_async_copy(a, a_out, sems.at[0]), pltpu.make_async_copy(b, b_out, sems.at[1])]
+    for copy in copies:
+        copy.start()
+    for copy in copies:
+        copy.wait()
 
 
 def per_device(n_row, n_col, kelvin, mass, labels, virgin, charred, residue, rate, energy, film, stag, elem, count):
@@ -434,11 +451,11 @@
     out, mass_out = pl.pallas_call(
         functools.partial(kernel, n_row, n_col, cx, cy, depth),
         out_shape=(whole, whole),
-        in_specs=[pl.BlockSpec(memory_space=pl.ANY)] * 12,
-        out_specs=(pl.BlockSpec(memory_space=pl.ANY),) * 2,
+        in_specs=[pl.BlockSpec(memory_space=pltpu.HBM)] * 12,
+        out_specs=(pl.BlockSpec(memory_space=pltpu.HBM),) * 2,
         scratch_shapes=scratch,
         compiler_params=pltpu.CompilerParams(
-            collective_id=0, has_side_effects=True, vmem_limit_bytes=24 * 1024 * 1024
+            collective_id=0, has_side_effects=True, vmem_limit_bytes=60 * 1024 * 1024
         ),
     )(
         kelvin.reshape(cells, depth), mass.reshape(cells, depth), labels,
@@ -446,6 +463,14 @@
         film.reshape(n_row, slots), stag.reshape(n_row, slots), elem.reshape(n_row, slots),
         count.reshape(1, n_row),
     )
+    out, mass_out = pl.pallas_call(
+        hand_over,
+        out_shape=(whole, whole),
+        in_specs=[pl.BlockSpec(memory_space=pltpu.HBM)] * 2,
+        out_specs=(pl.BlockSpec(memory_space=pltpu.HBM),) * 2,
+        scratch_shapes=[pltpu.SemaphoreType.DMA((2,))],
+        compiler_params=pltpu.CompilerParams(vmem_limit_bytes=60 * 1024 * 1024),
+    )(out, mass_out)
     return out.reshape(kelvin.shape), mass_out.reshape(kelvin.shape)
 
 

time: 64.5 us -> 79.5 us (1.23)
  Pallas kernels: 57.1 us -> 78.7 us
  local copies, waits for them, and re-layouts: 6.27 us -> 0 us
    pallas_call x0 -> x1, Pallas kernels: none -> 17 us  [per_device(): pl.pallas_call(hand_over, out_shape=(whole, whole), in_specs=[pl.BlockSpe...]
    unnamed x26 -> x0, local copies, waits for them, and re-layouts: 6.27 us -> none
    pallas_call x1, Pallas kernels: 57.1 us -> 61.7 us  [per_device(): pl.pallas_call(functools.partial(kernel, n_row, n_col, cx, cy, depth), ou...]
where the time goes in v2:
time: 79.5 us; the launch traced here: 79.4 us
  Pallas kernels  78.7 us (99%)
    pallas_call x1, Pallas kernels, per_device(): pl.pallas_call(functools.partial(kernel, n_row, n_col, cx, cy, depth), ou...  61.7 us
    pallas_call x1, Pallas kernels, per_device(): pl.pallas_call(hand_over, out_shape=(whole, whole), in_specs=[pl.BlockSpe...  17 us

profile of v2, /device:TPU:1, one launch (start us, length us, event | category | flops | bytes accessed | tf_op | source)
XLA Modules:
  0.0 79.4 jit_solution(8700275140762052694)
XLA Ops:
  0.6 61.7 %shard_map.131 = (f32[512,128]{1,0:T(8,128)}, f32[512,128]{1,0:T(8,128)}) custom-call(f32[512,128]{1,0:T(8,128)} %bitcast.8, f32[512,128]{1,0:T(8,128)} %bitcast.9, s32[8,64]{1,0:T(8,128)} %lab_h.1, f32[8]{0:T(128)} %virgin_h.1, f32[8]{0:T(128)} %charred_h.1, f32[8]{0:T(128)} %residue_h.1, f32[8]{0:T(128)} %rate_h.1, f32[8]{0:T(128)} %energy_h.1, ...), custom_call_target="tpu_custom_call" | custom-call | tf_op jit(solution)/shard_map/pallas_call | solution.py:451
  62.4 17.0 %shard_map.132 = (f32[512,128]{1,0:T(8,128)}, f32[512,128]{1,0:T(8,128)}) custom-call(f32[512,128]{1,0:T(8,128)} %get-tuple-element.6.a, f32[512,128]{1,0:T(8,128)} %get-tuple-element.7.b), custom_call_target="tpu_custom_call" | custom-call | tf_op jit(solution)/shard_map/pallas_call | solution.py:466

commit v3 on v2

--- a/solution.py
+++ b/solution.py
@@ -17,9 +17,9 @@
 F32 = jnp.float32
 BF16 = jnp.bfloat16
 
-N_X = 4
-FACE_ROWS = 3
+FACE_ROWS = 4
 PORT_ROWS = 5
+EARLY_PLANES = 3
 BACK_ROWS = 2
 
 
@@ -27,21 +27,21 @@
     n_row, n_col, cx, cy, depth,
     kel_h, mass_h, lab_h, virgin_h, charred_h, residue_h, rate_h, energy_h,
     film_h, stag_h, elem_h, count_h,
-    out_h, mass_out_h,
+    py_h, qy_h, ry_h, ends_h, mass_out_h,
     kel, mass, lab, virgin_s, charred_s, residue_s, rate_s, energy_s,
     film, stag, elem, count,
     props, sol_u, sol_v, first_u, first_v,
     face_s, face_r, split, cond, mass2, rhs,
-    k_row_s, k_row_r, k_col_s, k_col_r,
+    lab_next, tops, k_col_s, k_col_r,
     gx, lx, px, port_s, port_r, back_s, back_r,
-    gy, dy, qy, ry, py, ypt_s, ypt_r, yrh_s, yrh_r, yfac, ysol, out,
+    gy, dy, qy, ry, py, ypt_s, ypt_r, yrh_s, yrh_r, yfac, ysol, ends,
     in_sem, out_sem, send_sem, recv_sem,
 ):
     row, col = lax.axis_index("row"), lax.axis_index("col")
 
     loads = [
         (film_h, film), (stag_h, stag), (elem_h, elem), (count_h, count),
-        (kel_h, kel), (mass_h, mass), (lab_h, lab),
+        (kel_h, kel.at[pl.ds(0, cx * cy), :]), (mass_h, mass.at[pl.ds(0, cx * cy), :]), (lab_h, lab),
         (virgin_h, virgin_s), (charred_h, charred_s), (residue_h, residue_s),
         (rate_h, rate_s), (energy_h, energy_s),
     ]
@@ -51,14 +51,8 @@
 
     barrier = pltpu.get_barrier_semaphore()
 
-    def far_first(n, size):
-        return lax.rem(size + size // 2 + (n + 1) // 2 * (1 - 2 * lax.rem(n, 2)), size)
-
-    n_z = n_row // N_X
-
     def row_peer(n):
-        x = lax.rem(row // n_z + far_first(lax.rem(n, N_X), N_X), N_X)
-        return x * n_z + lax.rem(lax.rem(row, n_z) + far_first(n // N_X, n_z), n_z)
+        return lax.rem(row + n + 1, n_row)
 
     def greet_row(n, _):
         pl.semaphore_signal(barrier, inc=1, device_id={"row": row_peer(n)}, device_id_type=MESH)
@@ -126,28 +120,59 @@
     weight = jnp.where(face_lane < counts, film[...], 0.0)
     strided(face_s, 0)[...] = weight
     strided(face_s, 1)[...] = jnp.where(face_lane < counts, weight * stag[...], 0.0)
-    strided(face_s, 2)[...] = elem[...].astype(F32)
+    place = elem[...].astype(F32)
+    strided(face_s, 2)[...] = place
+    place_x = jnp.floor(place * (1.0 / cy))
+    split[5] = place - place_x * cy
+    for j, value in enumerate((weight, weight * stag[...])):
+        value = jnp.where((face_lane < counts) & (place_x == 0.0), value, 0.0)
+        high = value.astype(BF16).astype(F32)
+        strided(tops, j)[...] = high
+        strided(tops, 2 + j)[...] = value - high
+        strided(tops, 4 + j)[...] = jnp.zeros(value.shape, F32)
+        strided(tops, 6 + j)[...] = jnp.zeros(value.shape, F32)
+    slots = film.shape[1]
+    x_index = lax.broadcasted_iota(jnp.int32, (cx, slots), 0).astype(F32)
+    y_index = lax.broadcasted_iota(jnp.int32, (cy, slots), 0).astype(F32)
+    contract_last = (((1,), (1,)), ((), ()))
+
+    def add_tops(tile, _):
+        right = jnp.where(y_index == split[5, pl.ds(tile, 1), :], 1.0, 0.0)
+        left = tops[pl.ds(pl.multiple_of(tile * 8, 8), 8), :]
+        sums = lax.dot_general(
+            left.astype(BF16), right.astype(BF16), contract_last, preferred_element_type=F32
+        )
+        pair = [sums[j : j + 1, :] + sums[2 + j : 3 + j, :] for j in range(2)]
+        if slots > 2 * cy:
+            pair.append(jnp.zeros((1, slots - 2 * cy), F32))
+        before = lax.rem(tile + n_row - 1, n_row)
+        face_s[pl.ds(before * 8 + 3, 1), :] = jnp.concatenate(pair, axis=1)
+        return 0
+
+    lax.fori_loop(0, n_row, add_tops, 0, unroll=16)
 
     for load in loads[4:]:
         load.wait()
-    zone = lab[...]
-
-    def look_up(table):
-        value = jnp.full(zone.shape, table[0], F32)
-        for z in range(1, 8):
-            value = jnp.where(zone == z, table[z], value)
-        return value
-
-    virgin, charred, residue = look_up(virgin_s), look_up(charred_s), look_up(residue_s)
-    slope = (virgin - charred) / (1.0 - residue)
-    table = jnp.concatenate(
-        [charred, slope, residue, look_up(rate_s), look_up(energy_s)], axis=0
-    ).T
-    for p in range(5):
-        for x in range(cx):
-            props[p, x * cy : (x + 1) * cy, :] = jnp.broadcast_to(
-                table[:, p * cx + x : p * cx + x + 1], (cy, depth)
-            )
+
+    def set_props(zone, start, planes):
+        def look_up(table):
+            value = jnp.full(zone.shape, table[0], F32)
+            for z in range(1, 8):
+                value = jnp.where(zone == z, table[z], value)
+            return value
+
+        virgin, charred, residue = look_up(virgin_s), look_up(charred_s), look_up(residue_s)
+        slope = (virgin - charred) / (1.0 - residue)
+        table = jnp.concatenate(
+            [charred, slope, residue, look_up(rate_s), look_up(energy_s)], axis=0
+        ).T
+        for p in range(5):
+            for x in range(planes):
+                props[p, (start + x) * cy : (start + x + 1) * cy, :] = jnp.broadcast_to(
+                    table[:, p * cx + x : p * cx + x + 1], (cy, depth)
+                )
+
+    set_props(lab[...], 0, cx)
 
     def depth_sweep(x, _):
         rows = pl.ds(pl.multiple_of(x * cy, cy), cy)
@@ -178,10 +203,32 @@
 
     first_u[...] = jnp.zeros(first_u.shape, F32)
     first_v[...] = jnp.zeros(first_v.shape, F32)
-    lax.fori_loop(0, cx, depth_sweep, 0)
-
+    def send_before(source, target, axis, position, size, phase):
+        copy = pltpu.make_async_remote_copy(
+            src_ref=source,
+            dst_ref=target,
+            send_sem=send_sem.at[phase],
+            recv_sem=recv_sem.at[phase],
+            device_id={axis: lax.rem(position + size - 1, size)},
+            device_id_type=MESH,
+        )
+        copy.start()
+        return copy
+
+    lax.fori_loop(0, EARLY_PLANES, depth_sweep, 0)
     pl.semaphore_wait(barrier, n_row - 1 + n_col - 1)
     exchange_row(face_s, face_r, FACE_ROWS, 0)
+    first_rows, extra_rows = pl.ds(0, cy), pl.ds(cx * cy, cy)
+    firsts = [
+        send_before(kel.at[first_rows, :], kel.at[extra_rows, :], "row", row, n_row, 1),
+        send_before(mass.at[first_rows, :], mass.at[extra_rows, :], "row", row, n_row, 7),
+        send_before(lab, lab_next, "row", row, n_row, 8),
+    ]
+    lax.fori_loop(EARLY_PLANES, cx, depth_sweep, 0)
+    for copy in firsts:
+        copy.wait_recv()
+    set_props(lab_next[...], cx, 1)
+    lax.fori_loop(cx, cx + 1, depth_sweep, 0)
 
     await_bytes(row_bytes(face_r, FACE_ROWS), recv_sem.at[0])
     for j in range(2):
@@ -193,9 +240,6 @@
     place_x = jnp.floor(place * (1.0 / cy))
     split[4] = place_x
     split[5] = place - place_x * cy
-    slots = film.shape[1]
-    x_index = lax.broadcasted_iota(jnp.int32, (cx, slots), 0).astype(F32)
-    y_index = lax.broadcasted_iota(jnp.int32, (cy, slots), 0).astype(F32)
 
     def add_faces(pair, total):
         lefts, rights = [], []
@@ -211,7 +255,7 @@
         left = jnp.concatenate(lefts, axis=1).astype(BF16)
         right = jnp.concatenate(rights, axis=1).astype(BF16)
         return total + lax.dot_general(
-            right, left, (((1,), (1,)), ((), ())), preferred_element_type=F32
+            right, left, contract_last, preferred_element_type=F32
         )
 
     sums = lax.fori_loop(0, n_row // 2, add_faces, jnp.zeros((cy, 4 * cx), F32), unroll=True)
@@ -223,34 +267,29 @@
         / (1.0 + EXTERIOR_SHARE * wall_w * first_v[:, 0:cx])
     )
 
-    def send_k(source, target, axis, position, size, phase):
-        copy = pltpu.make_async_remote_copy(
-            src_ref=source,
-            dst_ref=target,
-            send_sem=send_sem.at[phase],
-            recv_sem=recv_sem.at[phase],
-            device_id={axis: lax.rem(position + size - 1, size)},
-            device_id_type=MESH,
-        )
-        copy.start()
-        return copy
-
-    for x in range(cx):
+    next_wall = jnp.broadcast_to(jnp.sum(strided(face_r, 3)[...], axis=0, keepdims=True), (8, slots)).T
+    next_w, next_q = next_wall[0:cy, 0:1], next_wall[cy : 2 * cy, 0:1]
+    next_alpha = (
+        EXTERIOR_SHARE
+        * (next_q - next_w * first_u[:, cx : cx + 1])
+        / (1.0 + EXTERIOR_SHARE * next_w * first_v[:, cx : cx + 1])
+    )
+
+    for x in range(cx + 1):
         rows = pl.ds(x * cy, cy)
         m = mass[rows, :]
         res = props[2, rows, :]
-        t = sol_u[rows, :] + alpha[:, x : x + 1] * sol_v[rows, :]
+        share = alpha[:, x : x + 1] if x < cx else next_alpha
+        t = sol_u[rows, :] + share * sol_v[rows, :]
         extent = props[3, rows, :] * jnp.exp(-props[4, rows, :] / t)
         excess = (m - res) * jnp.exp(-extent)
-        m2 = res + excess
-        mass2[rows, :] = m2
-        rhs[rows, :] = m2 * t - HEAT_OF_PYROLYSIS * (m - m2)
         cond[rows, :] = props[0, rows, :] + props[1, rows, :] * excess
-        if x == 0:
-            k_row_s[...] = cond[rows, :]
-            k_row = send_k(k_row_s, k_row_r, "row", row, n_row, 1)
+        if x < cx:
+            m2 = res + excess
+            mass2[rows, :] = m2
+            rhs[rows, :] = m2 * t - HEAT_OF_PYROLYSIS * (m - m2)
     k_col_s[...] = cond[pl.ds(0, cx, stride=cy), :]
-    k_col = send_k(k_col_s, k_col_r, "col", col, n_col, 2)
+    k_col = send_before(k_col_s, k_col_r, "col", col, n_col, 2)
 
     def plane(ref, x):
         return ref[pl.ds(x * cy, cy), :]
@@ -260,11 +299,8 @@
     left_rhs = plane(rhs, 0)
     coupling, held, right_hand = face, face, plane(rhs, 1)
     for x in range(1, cx):
-        if x < cx - 1:
-            face = (0.5 * R_X) * (plane(cond, x) + plane(cond, x + 1))
-        else:
-            k_row.wait_recv()
-            face = (0.5 * R_X) * (plane(cond, x) + k_row_r[...])
+        face = (0.5 * R_X) * (plane(cond, x) + plane(cond, x + 1))
+        if x == cx - 1:
             face = jnp.where(row == n_row - 1, 0.0, face)
         inv = 1.0 / (plane(mass2, x) + held + face)
         g, l, p = face * inv, coupling * inv, right_hand * inv
@@ -306,8 +342,13 @@
     ypt_s[0], ypt_s[1], ypt_s[2] = left, -coupling, held
     exchange_col(ypt_s, ypt_r, 4)
 
-    mass_out = pltpu.make_async_copy(mass2, mass_out_h, out_sem.at[0])
-    mass_out.start()
+    stores = [
+        pltpu.make_async_copy(a, b, out_sem.at[i])
+        for i, (a, b) in enumerate(
+            [(mass2, mass_out_h), (qy, qy_h), (ry, ry_h), (py, py_h), (ends, ends_h)]
+        )
+    ]
+    stores[0].start()
 
     await_bytes(row_bytes(port_r, PORT_ROWS), recv_sem.at[3])
     down = strided(port_r, 1)[...]
@@ -340,6 +381,8 @@
     zero = jnp.zeros((cx, depth), F32)
     lax.fori_loop(0, cy - 1, answer_y, (zero, zero + 1.0), unroll=7)
     qy[0], ry[0] = zero + 1.0, zero
+    stores[1].start()
+    stores[2].start()
 
     await_bytes(ypt_r.at[pl.ds(0, n_col - 1)], recv_sem.at[4])
     diag = ypt_r[0, 0]
@@ -381,6 +424,7 @@
     lax.fori_loop(1, cy, forward_y, zero, unroll=7)
     lax.fori_loop(0, cy - 1, backward_y, zero, unroll=7)
     py[0] = zero
+    stores[3].start()
 
     await_bytes(yrh_r.at[pl.ds(0, n_col - 1)], recv_sem.at[6])
     value = yrh_r[0, 0]
@@ -394,33 +438,41 @@
     for i in range(n_col - 2, -1, -1):
         value = ysol[i] * yfac[0, i] - yfac[1, i] * value
         ysol[i] = value
-    y_first, y_next = ysol[col], ysol[col + 1]
-
-    def finish(y, _):
-        out[pl.ds(y, cx, stride=cy), :] = py[y] + qy[y] * y_first + ry[y] * y_next
-        return 0
-
-    lax.fori_loop(0, cy, finish, 0, unroll=8)
-    result = pltpu.make_async_copy(out, out_h, out_sem.at[1])
-    result.start()
+    ends[0], ends[1] = ysol[col], ysol[col + 1]
+    stores[4].start()
 
     await_bytes(row_bytes(face_s, FACE_ROWS), send_sem.at[0])
-    k_row.wait_send()
+    for copy in firsts:
+        copy.wait_send()
     k_col.wait_send()
     await_bytes(row_bytes(port_s, PORT_ROWS), send_sem.at[3])
     await_bytes(ypt_r.at[pl.ds(0, n_col - 1)], send_sem.at[4])
     await_bytes(row_bytes(back_s, BACK_ROWS), send_sem.at[5])
     await_bytes(yrh_r.at[pl.ds(0, n_col - 1)], send_sem.at[6])
+    for store in stores:
+        store.wait()
+
+
+def finish(cx, cy, py_h, qy_h, ry_h, ends_h, mass_h, out_h, mass_out_h, py, qy, ry, ends, mass, out, sems):
+    pairs = [(ends_h, ends), (py_h, py), (qy_h, qy), (ry_h, ry), (mass_h, mass)]
+    loads = [pltpu.make_async_copy(a, b, sems.at[i]) for i, (a, b) in enumerate(pairs)]
+    for load in loads:
+        load.start()
+    for load in loads:
+        load.wait()
+    mass_out = pltpu.make_async_copy(mass, mass_out_h, sems.at[5])
+    mass_out.start()
+    first, after = ends[0], ends[1]
+
+    def cells(y, _):
+        out[pl.ds(y, cx, stride=cy), :] = py[y] + qy[y] * first + ry[y] * after
+        return 0
+
+    lax.fori_loop(0, cy, cells, 0, unroll=16)
+    result = pltpu.make_async_copy(out, out_h, sems.at[6])
+    result.start()
     mass_out.wait()
     result.wait()
-
-
-def hand_over(a, b, a_out, b_out, sems):
-    copies = [pltpu.make_async_copy(a, a_out, sems.at[0]), pltpu.make_async_copy(b, b_out, sems.at[1])]
-    for copy in copies:
-        copy.start()
-    for copy in copies:
-        copy.wait()
 
 
 def per_device(n_row, n_col, kelvin, mass, labels, virgin, charred, residue, rate, energy, film, stag, elem, count):
@@ -430,29 +482,31 @@
     vmem = lambda *shape: pltpu.VMEM(shape, F32)
     zones = virgin.shape[0]
     scratch = [
-        vmem(cells, depth), vmem(cells, depth), pltpu.VMEM((cx, cy), jnp.int32),
+        vmem(cells + cy, depth), vmem(cells + cy, depth), pltpu.VMEM((cx, cy), jnp.int32),
         *[pltpu.SMEM((zones,), F32)] * 5,
         vmem(n_row, slots), vmem(n_row, slots), pltpu.VMEM((n_row, slots), jnp.int32),
         pltpu.VMEM((1, n_row), jnp.int32),
-        vmem(5, cells, depth), vmem(cells, depth), vmem(cells, depth), vmem(cy, depth), vmem(cy, depth),
+        vmem(5, cells + cy, depth), vmem(cells + cy, depth), vmem(cells + cy, depth), vmem(cy, depth), vmem(cy, depth),
         vmem(n_row * 8, slots), vmem(n_row * 8, slots), vmem(6, n_row, slots),
-        vmem(cells, depth), vmem(cells, depth), vmem(cells, depth),
-        vmem(cy, depth), vmem(cy, depth), vmem(cx, depth), vmem(cx, depth),
+        vmem(cells + cy, depth), vmem(cells, depth), vmem(cells, depth),
+        pltpu.VMEM((cx, cy), jnp.int32), vmem(n_row * 8, slots), vmem(cx, depth), vmem(cx, depth),
         vmem(cx, cy, depth), vmem(cx, cy, depth), vmem(cx, cy, depth),
         *[vmem(n_row * 8, depth)] * 4,
         *[vmem(cy, cx, depth)] * 5,
         vmem(3, cx, depth), vmem(n_col, 3, cx, depth),
         vmem(2, cx, depth), vmem(n_col, 2, cx, depth),
-        vmem(2, n_col, cx, depth), vmem(n_col + 1, cx, depth), vmem(cells, depth),
-        pltpu.SemaphoreType.DMA((12,)), pltpu.SemaphoreType.DMA((2,)),
-        pltpu.SemaphoreType.DMA((7,)), pltpu.SemaphoreType.DMA((7,)),
+        vmem(2, n_col, cx, depth), vmem(n_col + 1, cx, depth), vmem(2, cx, depth),
+        pltpu.SemaphoreType.DMA((12,)), pltpu.SemaphoreType.DMA((5,)),
+        pltpu.SemaphoreType.DMA((9,)), pltpu.SemaphoreType.DMA((9,)),
     ]
+    hbm = pl.BlockSpec(memory_space=pltpu.HBM)
     whole = jax.ShapeDtypeStruct((cells, depth), F32)
-    out, mass_out = pl.pallas_call(
+    lines = jax.ShapeDtypeStruct((cy, cx, depth), F32)
+    parts = pl.pallas_call(
         functools.partial(kernel, n_row, n_col, cx, cy, depth),
-        out_shape=(whole, whole),
-        in_specs=[pl.BlockSpec(memory_space=pltpu.HBM)] * 12,
-        out_specs=(pl.BlockSpec(memory_space=pltpu.HBM),) * 2,
+        out_shape=(lines, lines, lines, jax.ShapeDtypeStruct((2, cx, depth), F32), whole),
+        in_specs=[hbm] * 12,
+        out_specs=(hbm,) * 5,
         scratch_shapes=scratch,
         compiler_params=pltpu.CompilerParams(
             collective_id=0, has_side_effects=True, vmem_limit_bytes=60 * 1024 * 1024
@@ -464,13 +518,16 @@
         count.reshape(1, n_row),
     )
     out, mass_out = pl.pallas_call(
-        hand_over,
+        functools.partial(finish, cx, cy),
         out_shape=(whole, whole),
-        in_specs=[pl.BlockSpec(memory_space=pltpu.HBM)] * 2,
-        out_specs=(pl.BlockSpec(memory_space=pltpu.HBM),) * 2,
-        scratch_shapes=[pltpu.SemaphoreType.DMA((2,))],
+        in_specs=[hbm] * 5,
+        out_specs=(hbm,) * 2,
+        scratch_shapes=[
+            *[vmem(cy, cx, depth)] * 3, vmem(2, cx, depth), vmem(cells, depth), vmem(cells, depth),
+            pltpu.SemaphoreType.DMA((7,)),
+        ],
         compiler_params=pltpu.CompilerParams(vmem_limit_bytes=60 * 1024 * 1024),
-    )(out, mass_out)
+    )(*parts)
     return out.reshape(kelvin.shape), mass_out.reshape(kelvin.shape)
 
 

time: 79.5 us -> 59.1 us (0.74)
  Pallas kernels: 78.7 us -> 58.3 us
    pallas_call x1, Pallas kernels: 17 us -> 2.14 us  [per_device(): pl.pallas_call(functools.partial(finish, cx, cy), out_shape=(whole, whole...]
    pallas_call x1, Pallas kernels: 61.7 us -> 56.2 us  [per_device(): pl.pallas_call(functools.partial(kernel, n_row, n_col, cx, cy, depth), ou...]
where the time goes in v3:
time: 59.1 us; the launch traced here: 59 us
  Pallas kernels  58.3 us (99%)
  between operations  0.64 us (1%)
    pallas_call x1, Pallas kernels, per_device(): pl.pallas_call(functools.partial(kernel, n_row, n_col, cx, cy, depth), ou...  56.2 us
    pallas_call x1, Pallas kernels, per_device(): pl.pallas_call(functools.partial(finish, cx, cy), out_shape=(whole, whole...  2.14 us

profile of v3, /device:TPU:1, one launch (start us, length us, event | category | flops | bytes accessed | tf_op | source)
XLA Modules:
  0.0 59.0 jit_solution(8895024761413799438)
XLA Ops:
  0.6 56.2 %shard_map.131 = (f32[64,8,128]{2,1,0:T(8,128)}, f32[64,8,128]{2,1,0:T(8,128)}, f32[64,8,128]{2,1,0:T(8,128)}, f32[2,8,128]{2,1,0:T(8,128)}, f32[512,128]{1,0:T(8,128)}) custom-call(f32[512,128]{1,0:T(8,128)} %bitcast.8, f32[512,128]{1,0:T(8,128)} %bitcast.9, s32[8,64]{1,0:T(8,128)} %lab_h.1, f32[8]{0:T(128)} %virgin_h.1, f32[8]{0:T(128)} %charred_h.1, ...), custom_call_target="tpu_custom_call" | custom-call | tf_op jit(solution)/shard_map/pallas_call | solution.py:505
  56.8 2.1 %shard_map.132 = (f32[512,128]{1,0:T(8,128)}, f32[512,128]{1,0:T(8,128)}) custom-call(f32[64,8,128]{2,1,0:T(8,128)} %get-tuple-element.9.py_h, f32[64,8,128]{2,1,0:T(8,128)} %get-tuple-element.10.qy_h, f32[64,8,128]{2,1,0:T(8,128)} %get-tuple-element.11.ry_h, f32[2,8,128]{2,1,0:T(8,128)} %get-tuple-element.12.ends_h, f32[512,128]{1,0:T(8,128)} %get-tuple-element.13.mass_h), custom_call_target="tpu_custom_call" | custom-call | tf_op jit(solution)/shard_map/pallas_call | solution.py:520

commit v4 on v3

--- a/solution.py
+++ b/solution.py
@@ -17,6 +17,7 @@
 F32 = jnp.float32
 BF16 = jnp.bfloat16
 
+N_X = 4
 FACE_ROWS = 4
 PORT_ROWS = 5
 EARLY_PLANES = 3
@@ -51,11 +52,17 @@
 
     barrier = pltpu.get_barrier_semaphore()
 
+    def far_first(n, size):
+        return lax.rem(size + size // 2 + (n + 1) // 2 * (1 - 2 * lax.rem(n, 2)), size)
+
+    n_z = n_row // N_X
+
     def row_peer(n):
-        return lax.rem(row + n + 1, n_row)
+        x = lax.rem(row // n_z + far_first(lax.rem(n, N_X), N_X), N_X)
+        return x * n_z + lax.rem(lax.rem(row, n_z) + far_first(n // N_X, n_z), n_z)
 
     def greet_row(n, _):
-        pl.semaphore_signal(barrier, inc=1, device_id={"row": row_peer(n)}, device_id_type=MESH)
+        pl.semaphore_signal(barrier, inc=1, device_id={"row": lax.rem(row + n + 1, n_row)}, device_id_type=MESH)
         return 0
 
     def greet_col(t, _):
@@ -217,13 +224,13 @@
 
     lax.fori_loop(0, EARLY_PLANES, depth_sweep, 0)
     pl.semaphore_wait(barrier, n_row - 1 + n_col - 1)
-    exchange_row(face_s, face_r, FACE_ROWS, 0)
     first_rows, extra_rows = pl.ds(0, cy), pl.ds(cx * cy, cy)
     firsts = [
         send_before(kel.at[first_rows, :], kel.at[extra_rows, :], "row", row, n_row, 1),
         send_before(mass.at[first_rows, :], mass.at[extra_rows, :], "row", row, n_row, 7),
         send_before(lab, lab_next, "row", row, n_row, 8),
     ]
+    exchange_row(face_s, face_r, FACE_ROWS, 0)
     lax.fori_loop(EARLY_PLANES, cx, depth_sweep, 0)
     for copy in firsts:
         copy.wait_recv()

time: 59.1 us -> 56.9 us (0.963)
  Pallas kernels: 58.3 us -> 56.1 us
    pallas_call x1, Pallas kernels: 56.2 us -> 53.9 us  [per_device(): pl.pallas_call(functools.partial(kernel, n_row, n_col, cx, cy, depth), ou...]
where the time goes in v4:
time: 56.9 us; the launch traced here: 56.7 us
  Pallas kernels  56.1 us (99%)
  between operations  0.64 us (1%)
    pallas_call x1, Pallas kernels, per_device(): pl.pallas_call(functools.partial(kernel, n_row, n_col, cx, cy, depth), ou...  53.9 us
    pallas_call x1, Pallas kernels, per_device(): pl.pallas_call(functools.partial(finish, cx, cy), out_shape=(whole, whole...  2.14 us

profile of v4, /device:TPU:1, one launch (start us, length us, event | category | flops | bytes accessed | tf_op | source)
XLA Modules:
  0.0 56.7 jit_solution(8095567030873029917)
XLA Ops:
  0.6 53.9 %shard_map.131 = (f32[64,8,128]{2,1,0:T(8,128)}, f32[64,8,128]{2,1,0:T(8,128)}, f32[64,8,128]{2,1,0:T(8,128)}, f32[2,8,128]{2,1,0:T(8,128)}, f32[512,128]{1,0:T(8,128)}) custom-call(f32[512,128]{1,0:T(8,128)} %bitcast.8, f32[512,128]{1,0:T(8,128)} %bitcast.9, s32[8,64]{1,0:T(8,128)} %lab_h.1, f32[8]{0:T(128)} %virgin_h.1, f32[8]{0:T(128)} %charred_h.1, ...), custom_call_target="tpu_custom_call" | custom-call | tf_op jit(solution)/shard_map/pallas_call | solution.py:512
  54.6 2.1 %shard_map.132 = (f32[512,128]{1,0:T(8,128)}, f32[512,128]{1,0:T(8,128)}) custom-call(f32[64,8,128]{2,1,0:T(8,128)} %get-tuple-element.9.py_h, f32[64,8,128]{2,1,0:T(8,128)} %get-tuple-element.10.qy_h, f32[64,8,128]{2,1,0:T(8,128)} %get-tuple-element.11.ry_h, f32[2,8,128]{2,1,0:T(8,128)} %get-tuple-element.12.ends_h, f32[512,128]{1,0:T(8,128)} %get-tuple-element.13.mass_h), custom_call_target="tpu_custom_call" | custom-call | tf_op jit(solution)/shard_map/pallas_call | solution.py:527

commit v5 on v4

--- a/solution.py
+++ b/solution.py
@@ -71,8 +71,8 @@
         )
         return 0
 
+    lax.fori_loop(1, n_col, greet_col, 0)
     lax.fori_loop(0, n_row - 1, greet_row, 0)
-    lax.fori_loop(1, n_col, greet_col, 0)
 
     lane = lax.broadcasted_iota(jnp.int32, (cy, depth), 1)
 

time: 56.9 us -> 56.4 us (level)
  no operation moved by 1% of the time
where the time goes in v5:
time: 56.4 us; the launch traced here: 56.3 us
  Pallas kernels  55.6 us (99%)
  between operations  0.64 us (1%)
    pallas_call x1, Pallas kernels, per_device(): pl.pallas_call(functools.partial(kernel, n_row, n_col, cx, cy, depth), ou...  53.5 us
    pallas_call x1, Pallas kernels, per_device(): pl.pallas_call(functools.partial(finish, cx, cy), out_shape=(whole, whole...  2.14 us

profile of v5, /device:TPU:1, one launch (start us, length us, event | category | flops | bytes accessed | tf_op | source)
XLA Modules:
  0.0 56.3 jit_solution(3736029765402217326)
XLA Ops:
  0.6 53.5 %shard_map.131 = (f32[64,8,128]{2,1,0:T(8,128)}, f32[64,8,128]{2,1,0:T(8,128)}, f32[64,8,128]{2,1,0:T(8,128)}, f32[2,8,128]{2,1,0:T(8,128)}, f32[512,128]{1,0:T(8,128)}) custom-call(f32[512,128]{1,0:T(8,128)} %bitcast.8, f32[512,128]{1,0:T(8,128)} %bitcast.9, s32[8,64]{1,0:T(8,128)} %lab_h.1, f32[8]{0:T(128)} %virgin_h.1, f32[8]{0:T(128)} %charred_h.1, ...), custom_call_target="tpu_custom_call" | custom-call | tf_op jit(solution)/shard_map/pallas_call | solution.py:512
  54.1 2.1 %shard_map.132 = (f32[512,128]{1,0:T(8,128)}, f32[512,128]{1,0:T(8,128)}) custom-call(f32[64,8,128]{2,1,0:T(8,128)} %get-tuple-element.9.py_h, f32[64,8,128]{2,1,0:T(8,128)} %get-tuple-element.10.qy_h, f32[64,8,128]{2,1,0:T(8,128)} %get-tuple-element.11.ry_h, f32[2,8,128]{2,1,0:T(8,128)} %get-tuple-element.12.ends_h, f32[512,128]{1,0:T(8,128)} %get-tuple-element.13.mass_h), custom_call_target="tpu_custom_call" | custom-call | tf_op jit(solution)/shard_map/pallas_call | solution.py:527

commit v6 on v5

--- a/solution.py
+++ b/solution.py
@@ -95,7 +95,7 @@
             ).start()
             return 0
 
-        lax.fori_loop(0, n_row - 1, send, 0)
+        lax.fori_loop(0, n_row - 1, send, 0, unroll=True)
         slot(target, row, rows)[...] = slot(source, row, rows)[...]
 
     def row_bytes(ref, rows):

time: 56.4 us -> 56.2 us (level)
  no operation moved by 1% of the time
where the time goes in v6:
time: 56.2 us; the launch traced here: 56.1 us
  Pallas kernels  55.4 us (99%)
  between operations  0.64 us (1%)
    pallas_call x1, Pallas kernels, per_device(): pl.pallas_call(functools.partial(kernel, n_row, n_col, cx, cy, depth), ou...  53.3 us
    pallas_call x1, Pallas kernels, per_device(): pl.pallas_call(functools.partial(finish, cx, cy), out_shape=(whole, whole...  2.14 us

profile of v6, /device:TPU:1, one launch (start us, length us, event | category | flops | bytes accessed | tf_op | source)
XLA Modules:
  0.0 56.1 jit_solution(11875917664499243031)
XLA Ops:
  0.6 53.3 %shard_map.131 = (f32[64,8,128]{2,1,0:T(8,128)}, f32[64,8,128]{2,1,0:T(8,128)}, f32[64,8,128]{2,1,0:T(8,128)}, f32[2,8,128]{2,1,0:T(8,128)}, f32[512,128]{1,0:T(8,128)}) custom-call(f32[512,128]{1,0:T(8,128)} %bitcast.8, f32[512,128]{1,0:T(8,128)} %bitcast.9, s32[8,64]{1,0:T(8,128)} %lab_h.1, f32[8]{0:T(128)} %virgin_h.1, f32[8]{0:T(128)} %charred_h.1, ...), custom_call_target="tpu_custom_call" | custom-call | tf_op jit(solution)/shard_map/pallas_call | solution.py:512
  53.9 2.1 %shard_map.132 = (f32[512,128]{1,0:T(8,128)}, f32[512,128]{1,0:T(8,128)}) custom-call(f32[64,8,128]{2,1,0:T(8,128)} %get-tuple-element.9.py_h, f32[64,8,128]{2,1,0:T(8,128)} %get-tuple-element.10.qy_h, f32[64,8,128]{2,1,0:T(8,128)} %get-tuple-element.11.ry_h, f32[2,8,128]{2,1,0:T(8,128)} %get-tuple-element.12.ends_h, f32[512,128]{1,0:T(8,128)} %get-tuple-element.13.mass_h), custom_call_target="tpu_custom_call" | custom-call | tf_op jit(solution)/shard_map/pallas_call | solution.py:527
